TPU v7x, 128 devices: a whole 4x4x4 slice. The times are simulated.
128 devices in a mesh: ab: 8 (over y_lo, z), cd: 16 (over x, y_hi, core).
Axes of the slice: x: 4, y: 4 (y_hi: 2, y_lo: 2; y = y_hi * 2 + y_lo), z: 4, core: 2. Of those that a mesh axis runs over, the one named last changes fastest.
Arguments:
- amplitudes: bfloat16 [1024, 51200], P('ab', 'cd'), may hold values from -6 to 6
- integrals: bfloat16 [16384, 51200], P('ab', 'cd'), may hold values from -0.078125 to 0.078125
- ab_sizes: int32 [8], replicated, may hold values from 1 to 4096, 16384 in all
- cd_sizes: int32 [8], replicated, may hold values from 1 to 12800, 51200 in all
- pair_index: int32 [1024], replicated, may hold values from 0 to 1023, each once
Outputs:
- ladder: float32 [1024, 16384], P(None, ('ab', 'cd'))
Inputs may be any that keep to these rules, and one draw needn't show every extreme that they name: `ab_sizes`: block sizes are positive and sum to 16384, the largest is exactly 4096. `cd_sizes`: block sizes are positive and sum to 51200, the largest is exactly 12800. `pair_index`: each residual row once.
All inputs are finite; a program needn't handle non-finite values.
Results may differ from a plain program's by a relative error of at most 0.0003.
Values may be sent and summed in bfloat16 or wider, within the bound.
A program may use at most 128 MiB of HBM per device.

v0:
```python
import jax
import jax.numpy as jnp
from jax import lax
from jax.sharding import PartitionSpec as P


def from_behind(x, axis, by):
    devices = lax.axis_size(axis)
    return lax.ppermute(x, axis, [(i, (i + by) % devices) for i in range(devices)])


def irrep_labels(sizes, start, count):
    ends = jnp.cumsum(sizes)
    where_at = start + jnp.arange(count, dtype=jnp.int32)
    return jnp.sum((where_at[:, None] >= ends[None, :]).astype(jnp.int32), axis=1)


def contract(panel, masked):
    return lax.dot_general(
        panel, masked, (((1,), (1,)), ((), ())), preferred_element_type=jnp.float32
    )


def sum_over_cd(result):
    return lax.psum_scatter(result, "cd", scatter_dimension=1, tiled=True)


def shards(amplitudes, integrals, ab_sizes, cd_sizes, pair_index):
    ab_rows, cd_cols = integrals.shape
    panel_rows = amplitudes.shape[0]
    cycle_size = lax.axis_size("ab")
    ab_me = lax.axis_index("ab")
    ab_label = irrep_labels(ab_sizes, ab_me * ab_rows, ab_rows)
    cd_label = irrep_labels(cd_sizes, lax.axis_index("cd") * cd_cols, cd_cols)
    masked = jnp.where(ab_label[:, None] == cd_label[None, :], integrals, jnp.zeros_like(integrals))
    all_pairs = pair_index.shape[0]
    current = amplitudes
    result = jnp.zeros((all_pairs, ab_rows), jnp.float32)
    for step in range(cycle_size):
        owner = (ab_me - step) % cycle_size
        targets = lax.dynamic_slice_in_dim(pair_index, owner * panel_rows, panel_rows)
        block = contract(current, masked)
        result = result.at[targets].set(block)
        if step + 1 < cycle_size:
            current = from_behind(current, "ab", 1)
    return sum_over_cd(result)


def solution(mesh):
    return jax.shard_map(
        shards,
        mesh=mesh,
        in_specs=(P("ab", "cd"), P("ab", "cd"), P(), P(), P()),
        out_specs=P(None, ("ab", "cd")),
        check_vma=False,
    )
```

profile of v0, /device:TPU:1, one launch (start us, length us, event | category | flops | bytes accessed | tf_op | source)
XLA Modules:
  0.0 274.1 jit_solution(4695899375874242989)
XLA Ops:
  6.5 2.5 collective-permute-start
  9.0 0.8 reduce-window.16
  9.8 0.8 reduce-window.17
  10.7 0.1 convert_reduce_fusion.1
  10.8 0.1 convert_reduce_fusion
  10.9 0.0 copy-start.2
  10.9 7.8 %compare_select_fusion = bf16[2048,3200]{1,0:T(8,128)(2,1)S(1)} fusion(bf16[2048,3200]{1,0:T(8,128)(2,1)} %param.6, s32[3200]{0:T(1024)S(1)} %convert_reduce_fusion, s32[2048]{0:T(1024)S(1)} %convert_reduce_fusion.1), kind=kLoop, calls=%fused_computation.8 | loop fusion | flops 13107200 | bytes 26235392 | tf_op jit(solution)/shard_map/jit(_where)/select_n | solution.py:35
  18.7 4.7 %copy-done = bf16[2048,3200]{1,0:T(8,128)(2,1)} copy-done((bf16[2048,3200]{1,0:T(8,128)(2,1)}, bf16[2048,3200]{1,0:T(8,128)(2,1)S(1)}, u32[]{:S(2)}) %copy-start) | copy-done | bytes 13107224
  23.4 3.8 %convolution_bitcast_fusion.7 = f32[128,2048]{0,1:T(8,128)S(1)} fusion(bf16[2048,3200]{1,0:T(8,128)(2,1)S(1)} %compare_select_fusion, bf16[128,3200]{1,0:T(8,128)(2,1)S(1)} %copy-done.2), kind=kOutput, calls=%fused_computation.18 | convolution fusion | flops 1677721600 | bytes 14974976 | tf_op jit(solution)/shard_map/dot_general | solution.py:19
  27.2 0.3 copy.14
  27.6 0.1 compare_select_fusion.1
  27.7 4.9 %scatter_custom_fusion = f32[1024,2048]{1,0:T(8,128)} fusion(s32[128]{0:T(128)S(1)} %get-tuple-element.11, f32[128,2048]{1,0:T(8,128)S(1)} %copy.14, f32[]{:T(128)} %constant.71.clone.1), kind=kCustom, calls=%fused_computation.9 | custom fusion | bytes 8388612 | tf_op jit(solution)/shard_map/scatter | solution.py:43
  32.6 0.0 collective-permute-done
  32.6 1.6 collective-permute-start.1
  34.2 6.8 %convolution_bitcast_fusion.6 = f32[128,2048]{0,1:T(8,128)S(1)} fusion(bf16[2048,3200]{1,0:T(8,128)(2,1)} %copy-done, bf16[128,3200]{1,0:T(8,128)(2,1)} %collective-permute-done), kind=kOutput, calls=%fused_computation.17 | convolution fusion | flops 1677721600 | bytes 14974976 | tf_op jit(solution)/shard_map/dot_general | solution.py:19
  41.1 0.3 copy.15
  41.4 7.8 %scatter_fusion = f32[1024,2048]{1,0:T(8,128)} fusion(f32[1024,2048]{1,0:T(8,128)} %scatter_custom_fusion, s32[128]{0:T(128)S(1)} %get-tuple-element.10, f32[128,2048]{1,0:T(8,128)S(1)} %copy.15), kind=kCustom, calls=%fused_computation.1 | custom fusion | bytes 3146240 | tf_op jit(solution)/shard_map/scatter | solution.py:43
  49.2 4.5 %collective-permute-done.1 = bf16[128,3200]{1,0:T(8,128)(2,1)S(1)} collective-permute-done((bf16[128,3200]{1,0:T(8,128)(2,1)}, bf16[128,3200]{1,0:T(8,128)(2,1)S(1)}, u32[]{:S(2)}, u32[]{:S(2)}) %collective-permute-start.1) | collective-permute-done | bytes 819232 | tf_op jit(solution)/shard_map/ppermute | solution.py:9
  53.7 0.0 collective-permute-start.2
  53.7 6.6 %convolution_bitcast_fusion.5 = f32[128,2048]{0,1:T(8,128)S(1)} fusion(bf16[2048,3200]{1,0:T(8,128)(2,1)} %copy-done, bf16[128,3200]{1,0:T(8,128)(2,1)S(1)} %collective-permute-done.1), kind=kOutput, calls=%fused_computation.16 | convolution fusion | flops 1677721600 | bytes 14974976 | tf_op jit(solution)/shard_map/dot_general | solution.py:19
  60.3 0.3 copy.16
  60.7 7.8 %scatter_fusion.1 = f32[1024,2048]{1,0:T(8,128)} fusion(f32[1024,2048]{1,0:T(8,128)} %scatter_fusion, s32[128]{0:T(128)S(1)} %get-tuple-element.9, f32[128,2048]{1,0:T(8,128)S(1)} %copy.16), kind=kCustom, calls=%fused_computation.2 | custom fusion | bytes 3146240 | tf_op jit(solution)/shard_map/scatter | solution.py:43
  68.4 5.4 %collective-permute-done.2 = bf16[128,3200]{1,0:T(8,128)(2,1)} collective-permute-done((bf16[128,3200]{1,0:T(8,128)(2,1)S(1)}, bf16[128,3200]{1,0:T(8,128)(2,1)}, u32[]{:S(2)}, u32[]{:S(2)}) %collective-permute-start.2) | collective-permute-done | bytes 819232 | tf_op jit(solution)/shard_map/ppermute | solution.py:9
  73.8 0.0 collective-permute-start.3
  73.8 6.8 %convolution_bitcast_fusion.4 = f32[128,2048]{0,1:T(8,128)S(1)} fusion(bf16[2048,3200]{1,0:T(8,128)(2,1)} %copy-done, bf16[128,3200]{1,0:T(8,128)(2,1)} %collective-permute-done.2), kind=kOutput, calls=%fused_computation.15 | convolution fusion | flops 1677721600 | bytes 14974976 | tf_op jit(solution)/shard_map/dot_general | solution.py:19
  80.6 0.3 copy.17
  81.0 7.8 %scatter_fusion.2 = f32[1024,2048]{1,0:T(8,128)} fusion(f32[1024,2048]{1,0:T(8,128)} %scatter_fusion.1, s32[128]{0:T(128)S(1)} %get-tuple-element.8, f32[128,2048]{1,0:T(8,128)S(1)} %copy.17), kind=kCustom, calls=%fused_computation.3 | custom fusion | bytes 3146240 | tf_op jit(solution)/shard_map/scatter | solution.py:43
  88.7 4.3 %collective-permute-done.3 = bf16[128,3200]{1,0:T(8,128)(2,1)S(1)} collective-permute-done((bf16[128,3200]{1,0:T(8,128)(2,1)}, bf16[128,3200]{1,0:T(8,128)(2,1)S(1)}, u32[]{:S(2)}, u32[]{:S(2)}) %collective-permute-start.3) | collective-permute-done | bytes 819232 | tf_op jit(solution)/shard_map/ppermute | solution.py:9
  93.0 0.0 collective-permute-start.4
  93.0 6.6 %convolution_bitcast_fusion.3 = f32[128,2048]{0,1:T(8,128)S(1)} fusion(bf16[2048,3200]{1,0:T(8,128)(2,1)} %copy-done, bf16[128,3200]{1,0:T(8,128)(2,1)S(1)} %collective-permute-done.3), kind=kOutput, calls=%fused_computation.14 | convolution fusion | flops 1677721600 | bytes 14974976 | tf_op jit(solution)/shard_map/dot_general | solution.py:19
  99.7 0.3 copy.18
  100.0 7.8 %scatter_fusion.3 = f32[1024,2048]{1,0:T(8,128)} fusion(f32[1024,2048]{1,0:T(8,128)} %scatter_fusion.2, s32[128]{0:T(128)S(1)} %get-tuple-element.7, f32[128,2048]{1,0:T(8,128)S(1)} %copy.18), kind=kCustom, calls=%fused_computation.4 | custom fusion | bytes 3146240 | tf_op jit(solution)/shard_map/scatter | solution.py:43
  107.8 3.5 %collective-permute-done.4 = bf16[128,3200]{1,0:T(8,128)(2,1)} collective-permute-done((bf16[128,3200]{1,0:T(8,128)(2,1)S(1)}, bf16[128,3200]{1,0:T(8,128)(2,1)}, u32[]{:S(2)}, u32[]{:S(2)}) %collective-permute-start.4) | collective-permute-done | bytes 819232 | tf_op jit(solution)/shard_map/ppermute | solution.py:9
  111.3 0.0 collective-permute-start.5
  111.3 6.8 %convolution_bitcast_fusion.2 = f32[128,2048]{0,1:T(8,128)S(1)} fusion(bf16[2048,3200]{1,0:T(8,128)(2,1)} %copy-done, bf16[128,3200]{1,0:T(8,128)(2,1)} %collective-permute-done.4), kind=kOutput, calls=%fused_computation.13 | convolution fusion | flops 1677721600 | bytes 14974976 | tf_op jit(solution)/shard_map/dot_general | solution.py:19
  118.1 0.3 copy.19
  118.5 7.8 %scatter_fusion.4 = f32[1024,2048]{1,0:T(8,128)} fusion(f32[1024,2048]{1,0:T(8,128)} %scatter_fusion.3, s32[128]{0:T(128)S(1)} %get-tuple-element.6, f32[128,2048]{1,0:T(8,128)S(1)} %copy.19), kind=kCustom, calls=%fused_computation.5 | custom fusion | bytes 3146240 | tf_op jit(solution)/shard_map/scatter | solution.py:43
  126.2 2.5 collective-permute-done.5
  128.7 0.0 collective-permute-start.6
  128.7 6.6 %convolution_bitcast_fusion.1 = f32[128,2048]{0,1:T(8,128)S(1)} fusion(bf16[2048,3200]{1,0:T(8,128)(2,1)} %copy-done, bf16[128,3200]{1,0:T(8,128)(2,1)S(1)} %collective-permute-done.5), kind=kOutput, calls=%fused_computation.12 | convolution fusion | flops 1677721600 | bytes 14974976 | tf_op jit(solution)/shard_map/dot_general | solution.py:19
  135.3 0.3 copy.20
  135.6 7.8 %scatter_fusion.5 = f32[1024,2048]{1,0:T(8,128)} fusion(f32[1024,2048]{1,0:T(8,128)} %scatter_fusion.4, s32[128]{0:T(128)S(1)} %get-tuple-element.12, f32[128,2048]{1,0:T(8,128)S(1)} %copy.20), kind=kCustom, calls=%fused_computation.6 | custom fusion | bytes 3146240 | tf_op jit(solution)/shard_map/scatter | solution.py:43
  143.4 2.1 collective-permute-done.6
  145.5 6.8 %convolution_bitcast_fusion = f32[128,2048]{0,1:T(8,128)S(1)} fusion(bf16[2048,3200]{1,0:T(8,128)(2,1)} %copy-done, bf16[128,3200]{1,0:T(8,128)(2,1)} %collective-permute-done.6), kind=kOutput, calls=%fused_computation.11 | convolution fusion | flops 1677721600 | bytes 14974976 | tf_op jit(solution)/shard_map/dot_general | solution.py:19
  152.3 0.3 copy.21
  152.7 7.8 %scatter_fusion.6 = f32[1024,2048]{1,0:T(8,128)} fusion(f32[1024,2048]{1,0:T(8,128)} %scatter_fusion.5, s32[128]{0:T(128)S(1)} %get-tuple-element.5, f32[128,2048]{1,0:T(8,128)S(1)} %copy.21), kind=kCustom, calls=%fused_computation.7 | custom fusion | bytes 3146240 | tf_op jit(solution)/shard_map/scatter | solution.py:43
  160.4 0.0 reduce-scatter.2.cloned.1.call-update
  160.5 106.8 %reduce-scatter.2.cloned.1.call-done = f32[1024,128]{1,0:T(8,128)} async-done(((f32[1024,2048]{1,0:T(8,128)}), f32[1024,128]{1,0:T(8,128)}) %reduce-scatter.2.cloned.1.call-update) | async-done | bytes 524304 | tf_op jit(solution)/shard_map/reduce_scatter | solution.py:25
  (7 shorter events, 0.0 us)
Async XLA Ops:
  6.5 260.7 %reduce-scatter.2.cloned.1.call-start = ((), (), s32[]{:S(2)}) async-start(), calls=%async_computation.1 | async-start | bytes 8912896 | tf_op jit(solution)/shard_map/reduce_scatter | solution.py:25
  6.5 26.1 %collective-permute-start = (bf16[128,3200]{1,0:T(8,128)(2,1)}, bf16[128,3200]{1,0:T(8,128)(2,1)}, u32[]{:S(2)}, u32[]{:S(2)}) collective-permute-start(bf16[128,3200]{1,0:T(8,128)(2,1)} %param.5), channel_id=1, source_target_pairs={{0,16},{16,32},{32,48},{48,64},{64,80},{80,96},{96,112},{112,0},{1... | collective-permute-start | bytes 2457608 | tf_op jit(solution)/shard_map/ppermute | solution.py:9
  10.9 12.5 %copy-start.2 = (bf16[128,3200]{1,0:T(8,128)(2,1)S(1)}, bf16[128,3200]{1,0:T(8,128)(2,1)}, u32[]{:S(2)}) copy-start(bf16[128,3200]{1,0:T(8,128)(2,1)} %param.5) | copy-start | bytes 2457604
  18.7 4.7 %copy-start = (bf16[2048,3200]{1,0:T(8,128)(2,1)}, bf16[2048,3200]{1,0:T(8,128)(2,1)S(1)}, u32[]{:S(2)}) copy-start(bf16[2048,3200]{1,0:T(8,128)(2,1)S(1)} %compare_select_fusion) | copy-start | bytes 39321604
  23.4 4.2 %copy-start.1 = (s32[1024]{0:T(1024)S(1)}, s32[1024]{0:T(1024)}, u32[]{:S(2)}) copy-start(s32[1024]{0:T(1024)} %param.9) | copy-start | bytes 12292
  32.6 21.1 %collective-permute-start.1 = (bf16[128,3200]{1,0:T(8,128)(2,1)}, bf16[128,3200]{1,0:T(8,128)(2,1)S(1)}, u32[]{:S(2)}, u32[]{:S(2)}) collective-permute-start(bf16[128,3200]{1,0:T(8,128)(2,1)} %collective-permute-done), channel_id=1, source_target_pairs={{0,16},{16,32},{32,48},{48,64},{64,80},{80,96},{96,112},{112,0},{1... | collective-permute-start | bytes 2457608 | tf_op jit(solution)/shard_map/ppermute | solution.py:9
  53.7 20.1 %collective-permute-start.2 = (bf16[128,3200]{1,0:T(8,128)(2,1)S(1)}, bf16[128,3200]{1,0:T(8,128)(2,1)}, u32[]{:S(2)}, u32[]{:S(2)}) collective-permute-start(bf16[128,3200]{1,0:T(8,128)(2,1)S(1)} %collective-permute-done.1), channel_id=1, source_target_pairs={{0,16},{16,32},{32,48},{48,64},{64,80},{80,96},{96,112},{112,0},{1... | collective-permute-start | bytes 2457608 | tf_op jit(solution)/shard_map/ppermute | solution.py:9
  73.8 19.3 %collective-permute-start.3 = (bf16[128,3200]{1,0:T(8,128)(2,1)}, bf16[128,3200]{1,0:T(8,128)(2,1)S(1)}, u32[]{:S(2)}, u32[]{:S(2)}) collective-permute-start(bf16[128,3200]{1,0:T(8,128)(2,1)} %collective-permute-done.2), channel_id=1, source_target_pairs={{0,16},{16,32},{32,48},{48,64},{64,80},{80,96},{96,112},{112,0},{1... | collective-permute-start | bytes 2457608 | tf_op jit(solution)/shard_map/ppermute | solution.py:9
  93.0 18.2 %collective-permute-start.4 = (bf16[128,3200]{1,0:T(8,128)(2,1)S(1)}, bf16[128,3200]{1,0:T(8,128)(2,1)}, u32[]{:S(2)}, u32[]{:S(2)}) collective-permute-start(bf16[128,3200]{1,0:T(8,128)(2,1)S(1)} %collective-permute-done.3), channel_id=1, source_target_pairs={{0,16},{16,32},{32,48},{48,64},{64,80},{80,96},{96,112},{112,0},{1... | collective-permute-start | bytes 2457608 | tf_op jit(solution)/shard_map/ppermute | solution.py:9
  111.3 17.4 %collective-permute-start.5 = (bf16[128,3200]{1,0:T(8,128)(2,1)}, bf16[128,3200]{1,0:T(8,128)(2,1)S(1)}, u32[]{:S(2)}, u32[]{:S(2)}) collective-permute-start(bf16[128,3200]{1,0:T(8,128)(2,1)} %collective-permute-done.4), channel_id=1, source_target_pairs={{0,16},{16,32},{32,48},{48,64},{64,80},{80,96},{96,112},{112,0},{1... | collective-permute-start | bytes 2457608 | tf_op jit(solution)/shard_map/ppermute | solution.py:9
  128.7 16.8 %collective-permute-start.6 = (bf16[128,3200]{1,0:T(8,128)(2,1)S(1)}, bf16[128,3200]{1,0:T(8,128)(2,1)}, u32[]{:S(2)}, u32[]{:S(2)}) collective-permute-start(bf16[128,3200]{1,0:T(8,128)(2,1)S(1)} %collective-permute-done.5), channel_id=1, source_target_pairs={{0,16},{16,32},{32,48},{48,64},{64,80},{80,96},{96,112},{112,0},{1... | collective-permute-start | bytes 2457608 | tf_op jit(solution)/shard_map/ppermute | solution.py:9
Sparse Core Ops, SparseCore 0:
  160.6 106.6 reduce-scatter.1
where the time goes:
time: 275 us; the launch traced here: 274 us
  waiting for transfers between devices  129 us (47%)
  local copies, waits for them, and re-layouts  66.6 us (24%)
  matrix products  51 us (19%)
  between operations  13.6 us (5%)
  other arithmetic  9.8 us (4%)
  starting transfers between devices  4.13 us (2%)
    reduce_scatter x1, waiting for transfers between devices, sum_over_cd(): return lax.psum_scatter(result, 'cd', scatter_dimension=1, tiled=True)  107 us
    scatter x8, local copies, waits for them, and re-layouts, shards(): result = result.at[targets].set(block)  59.3 us
    dot_general x8, matrix products, contract(): lax.dot_general(panel, masked, (((1,), (1,)), ((), ())), preferred_elemen...  51 us
    ppermute x7, waiting for transfers between devices, from_behind(): lax.ppermute(x, axis, [(i, (i + by) % devices) for i in range(devices)])  22.2 us
    select_n x1, other arithmetic, shards(): jnp.where(ab_label[:, None] == cd_label[None, :], integrals, jnp.zeros_li...  7.84 us
  transfers between devices with their start and end apart: 8, of which 7 were waited for; matrix products, arithmetic and copies ran while one was open for 39% of the time, Pallas kernels for 0%

commit v1 on v0

v1 whole, which is shorter than its diff:
```python
import functools

import jax
import jax.numpy as jnp
from jax import lax
from jax.experimental import pallas as pl
from jax.experimental.pallas import tpu as pltpu
from jax.sharding import PartitionSpec as P

MESH = pl.DeviceIdType.MESH
BF16, F32, I32 = jnp.bfloat16, jnp.float32, jnp.int32

PANELS = 8
LANES = 128
CHUNK = 16
DX = (2, 1, 3, 0)
AHEAD = 1

CROSS = 8
CUT = 13
CUT_REST = 16

GROUPS = ((0, 1), (1, 1), (2, 2), (4, 2), (6, 1), (7, 1))
SLOTS = {
    1: (("T00", "T01"), ("T02", "T03")),
    2: (("T10", "T11"), ("R05", "T12", "T13")),
    3: (("R06",), ("R15",)),
    4: (("R16", "T20"), ("T21",)),
    5: (("T22",), ("T23",)),
    6: (("T30", "T31", "R25"), ("T32", "T33", "R26")),
    7: (("T40", "T41", "R35"), ("T42", "T43", "R36")),
}
TAIL = ("T50", "T51", "R45", "T52", "T53", "R46", "R55", "R56")


def kernel(
    ab_sizes, cd_sizes, pairs_ref, amps_ref, ints_ref, out_ref,
    amps, ints, prod, from_core, x_one, x_two, from_y, cd_lab,
    g_send, g_recv, r_send, r_recv, local_sem,
):
    panel_rows, depth = amps_ref.shape
    ab_rows = ints_ref.shape[0]
    rounds = panel_rows // CHUNK
    lane_tiles = depth // LANES
    round_rows = PANELS * CHUNK

    ab, cd = lax.axis_index("ab"), lax.axis_index("cd")
    yl, z = ab // 4, lax.rem(ab, 4)
    x, yh, core = cd // 4, lax.rem(cd // 2, 2), lax.rem(cd, 2)
    z_up, z_down, z_far = lax.rem(z + 1, 4), lax.rem(z + 3, 4), lax.rem(z + 2, 4)
    mine, other = yl * 4, (1 - yl) * 4

    to_pair = {"ab": other + z, "cd": cd}
    to_up = {"ab": mine + z_up, "cd": cd}
    to_down = {"ab": mine + z_down, "cd": cd}
    to_core = {"ab": ab, "cd": x * 4 + yh * 2 + (1 - core)}
    to_y = {"ab": ab, "cd": x * 4 + (1 - yh) * 2 + core}
    to_right = {"ab": ab, "cd": lax.rem(x + 1, 4) * 4 + yh * 2 + core}
    to_left = {"ab": ab, "cd": lax.rem(x + 3, 4) * 4 + yh * 2 + core}

    def ints_copy(block):
        dx, dc, dy = DX[block // 4], 1 - (block // 2) % 2, block % 2
        part = lax.rem(x + dx, 4) * 4 + (yh + dy - 2 * yh * dy) * 2 + (core + dc - 2 * core * dc)
        start = pl.multiple_of(part * LANES, LANES)
        copy = pltpu.make_async_copy(
            ints_ref.at[pl.ds(start, LANES), :],
            ints.at[pl.ds(block * LANES, LANES), :],
            local_sem.at[block],
        )
        return copy, start

    blocks = ab_rows // LANES
    for block in range(blocks):
        ints_copy(block)[0].start()

    barrier = pltpu.get_barrier_semaphore()
    neighbours = (to_pair, to_up, to_down, to_core, to_y, to_right, to_left)
    for neighbour in neighbours:
        pl.semaphore_signal(barrier, inc=1, device_id=neighbour, device_id_type=MESH)
    pl.semaphore_wait(barrier, len(neighbours))

    def slot(q, owner, low, high):
        start = pl.multiple_of(q * round_rows + owner * CHUNK, CHUNK)
        return amps.at[pl.ds(start, CHUNK), pl.ds(low * LANES, (high - low) * LANES)]

    full, cross, rest = (0, lane_tiles), (0, CROSS), (CROSS, lane_tiles)
    low_cut, high_cut = (0, CUT), (CUT, lane_tiles)
    low_rest, high_rest = (CROSS, CUT_REST), (CUT_REST, lane_tiles)
    me, up, down, far = mine + z, mine + z_up, mine + z_down, mine + z_far
    o_me, o_up, o_down, o_far = other + z, other + z_up, other + z_down, other + z_far
    kinds = (
        (me, full, to_pair, o_me),
        (me, full, to_up, down),
        (me, full, to_down, up),
        (o_me, rest, to_up, o_down),
        (o_me, rest, to_down, o_up),
        (down, low_cut, to_up, far),
        (up, high_cut, to_down, far),
        (down, cross, to_pair, o_down),
        (up, cross, to_pair, o_up),
        (o_down, low_rest, to_up, o_far),
        (o_up, high_rest, to_down, o_far),
        (far, cross, to_pair, o_far),
    )

    def g_out(q, kind):
        owner, columns, target, _ = kinds[kind]
        ref = slot(q, owner, *columns)
        return pltpu.make_async_remote_copy(
            src_ref=ref, dst_ref=ref, send_sem=g_send.at[kind, q], recv_sem=g_recv.at[kind, q],
            device_id=target, device_id_type=MESH,
        )

    def g_in(q, kind):
        _, columns, target, owner = kinds[kind]
        ref = slot(q, owner, *columns)
        return pltpu.make_async_remote_copy(
            src_ref=ref, dst_ref=ref, send_sem=g_send.at[kind, q], recv_sem=g_recv.at[kind, q],
            device_id=target, device_id_type=MESH,
        )

    def first(q):
        if q < rounds:
            for kind in (1, 2, 0):
                g_out(q, kind).start()

    def second(q):
        g_in(q, 1).wait_recv()
        g_out(q, 5).start()
        g_out(q, 7).start()
        g_in(q, 2).wait_recv()
        g_out(q, 6).start()
        g_out(q, 8).start()
        g_in(q, 0).wait_recv()
        g_out(q, 3).start()
        g_out(q, 4).start()

    def third(q):
        g_in(q, 5).wait_recv()
        g_out(q, 11).start()
        g_in(q, 3).wait_recv()
        g_out(q, 9).start()
        g_in(q, 4).wait_recv()
        g_out(q, 10).start()

    def arrived(q):
        for kind in (6, 7, 8, 9, 10, 11):
            g_in(q, kind).wait_recv()

    for q in range(rounds):
        amps[pl.ds(pl.multiple_of(q * round_rows + me * CHUNK, CHUNK), CHUNK), :] = (
            amps_ref[pl.ds(q * CHUNK, CHUNK), :]
        )
    for q in range(1 + AHEAD):
        first(q)

    def ends(sizes):
        out, total = [], jnp.int32(0)
        for k in range(sizes.shape[0]):
            total = total + sizes[k]
            out.append(total)
        return out

    def labels(where_at, limits):
        label = jnp.zeros(where_at.shape, I32)
        for limit in limits:
            label = label + (where_at >= limit).astype(I32)
        return label.astype(F32).astype(BF16)

    ab_ends, cd_ends = ends(ab_sizes), ends(cd_sizes)
    cd_lab[...] = labels(cd * depth + lax.broadcasted_iota(I32, cd_lab.shape, 1), cd_ends)

    def mask(block):
        copy, start = ints_copy(block)
        copy.wait()
        at = lax.broadcasted_iota(I32, (LANES, LANES), 0) + (ab * ab_rows + start)
        ab_lab = labels(at, ab_ends)

        def one(k, carry):
            columns = pl.ds(pl.multiple_of(k * LANES, LANES), LANES)
            rows = pl.ds(block * LANES, LANES)
            here = jnp.broadcast_to(cd_lab[0:1, columns], (LANES, LANES))
            tile = ints[rows, columns]
            ints[rows, columns] = jnp.where(ab_lab == here, tile, jnp.zeros_like(tile))
            return carry

        lax.fori_loop(0, lane_tiles, one, 0)

    wide = 4 * LANES
    half = 2 * LANES

    def r_copy(g, kind, src, dst, target):
        return pltpu.make_async_remote_copy(
            src_ref=src, dst_ref=dst, send_sem=r_send.at[kind, g], recv_sem=r_recv.at[kind, g],
            device_id=target, device_id_type=MESH,
        )

    def rows_of(g):
        begin, count = GROUPS[g]
        return pl.ds(begin * round_rows, count * round_rows)

    def core_copy(g, k):
        rows = rows_of(g)
        return r_copy(
            g, k, prod.at[rows, pl.ds(k * wide, half)], from_core.at[rows, pl.ds(k * half, half)], to_core
        )

    def x_one_copy(g, way):
        rows = rows_of(g)
        return r_copy(
            g, 4 + way, prod.at[rows, pl.ds(half + way * LANES, LANES)], x_one.at[way, rows, :],
            (to_right, to_left)[way],
        )

    def x_two_copy(g, way):
        rows = rows_of(g)
        return r_copy(
            g, 6 + way, prod.at[rows, pl.ds((1 + way) * wide + half, half)], x_two.at[way, rows, :],
            (to_right, to_left)[way],
        )

    def y_copy(g):
        rows = rows_of(g)
        return r_copy(g, 8, prod.at[rows, pl.ds(3 * wide + half + LANES, LANES)], from_y.at[rows, :], to_y)

    def kept(k):
        return pl.ds(k * wide + half, half)

    def tile(g, k):
        rows = rows_of(g)
        prod[rows, pl.ds(k * wide, wide)] = lax.dot_general(
            amps[rows, :], ints[pl.ds(k * wide, wide), :], (((1,), (1,)), ((), ())),
            preferred_element_type=F32,
        )
        core_copy(g, k).start()
        if k == 1:
            core_copy(g, 0).wait_recv()
            prod[rows, kept(0)] += from_core[rows, pl.ds(0, half)]
            x_one_copy(g, 0).start()
            x_one_copy(g, 1).start()
        if k == 3:
            for way in range(2):
                core_copy(g, 1 + way).wait_recv()
                prod[rows, kept(1 + way)] += from_core[rows, pl.ds((1 + way) * half, half)]
                x_one_copy(g, way).wait_recv()
                prod[rows, pl.ds((1 + way) * wide + half + way * LANES, LANES)] += x_one[way, rows, :]
                x_two_copy(g, way).start()

    def sum_x(g):
        rows = rows_of(g)
        core_copy(g, 3).wait_recv()
        total = prod[rows, kept(3)] + from_core[rows, pl.ds(3 * half, half)]
        x_two_copy(g, 0).wait_recv()
        x_two_copy(g, 1).wait_recv()
        prod[rows, kept(3)] = total + x_two[0, rows, :] + x_two[1, rows, :]
        y_copy(g).start()

    def place(g):
        begin, count = GROUPS[g]
        y_copy(g).wait_recv()
        for q in range(begin, begin + count):
            rows = pl.ds(q * round_rows, round_rows)
            found = prod[rows, pl.ds(3 * wide + half, LANES)] + from_y[rows, :]
            high = found.astype(BF16)
            left = found - high.astype(F32)
            mid = left.astype(BF16)
            low = (left - mid.astype(F32)).astype(BF16)
            target = jnp.broadcast_to(pairs_ref[pl.ds(q, 1), :], out_ref.shape)
            goes = lax.broadcasted_iota(I32, out_ref.shape, 0) == target
            goes = jnp.where(goes, 1.0, 0.0).astype(BF16)
            term = jnp.dot(
                jnp.concatenate([goes, goes, goes], axis=1),
                jnp.concatenate([high, mid, low], axis=0),
                preferred_element_type=F32,
            )
            if q == 0:
                out_ref[...] = term
            else:
                out_ref[...] += term

    def run(steps):
        for step in steps:
            g, k = int(step[1]), int(step[2])
            if step[0] == "T":
                tile(g, k)
            elif k == 5:
                sum_x(g)
            else:
                place(g)

    for block in range(blocks // 2):
        mask(block)
    second(0)
    first(1 + AHEAD)
    for block in range(blocks // 2, blocks):
        mask(block)
    third(0)
    arrived(0)
    for q in range(1, rounds):
        second(q)
        first(q + 1 + AHEAD)
        run(SLOTS[q][0])
        third(q)
        run(SLOTS[q][1])
        arrived(q)
    run(TAIL)

    for q in range(rounds):
        for kind in range(len(kinds)):
            g_out(q, kind).wait_send()
    for g in range(len(GROUPS)):
        for k in range(4):
            core_copy(g, k).wait_send()
        for way in range(2):
            x_one_copy(g, way).wait_send()
            x_two_copy(g, way).wait_send()
        y_copy(g).wait_send()


def shards(amplitudes, integrals, ab_sizes, cd_sizes, pair_index):
    panel_rows, depth = amplitudes.shape
    ab_rows = integrals.shape[0]
    all_pairs = pair_index.shape[0]
    rounds = panel_rows // CHUNK
    keeps = ab_rows // lax.axis_size("cd")
    pairs = pair_index.reshape(PANELS, rounds, CHUNK).transpose(1, 0, 2).reshape(rounds, PANELS * CHUNK)
    vmem, smem = pl.BlockSpec(memory_space=pltpu.VMEM), pl.BlockSpec(memory_space=pltpu.SMEM)
    return pl.pallas_call(
        kernel,
        out_shape=jax.ShapeDtypeStruct((all_pairs, keeps), F32),
        in_specs=[smem, smem, vmem, vmem, pl.BlockSpec(memory_space=pl.ANY)],
        out_specs=vmem,
        scratch_shapes=[
            pltpu.VMEM((all_pairs, depth), BF16),
            pltpu.VMEM((ab_rows, depth), BF16),
            pltpu.VMEM((all_pairs, ab_rows), F32),
            pltpu.VMEM((all_pairs, ab_rows // 2), F32),
            pltpu.VMEM((2, all_pairs, keeps), F32),
            pltpu.VMEM((2, all_pairs, 2 * keeps), F32),
            pltpu.VMEM((all_pairs, keeps), F32),
            pltpu.VMEM((16, depth), BF16),
            pltpu.SemaphoreType.DMA((12, rounds)),
            pltpu.SemaphoreType.DMA((12, rounds)),
            pltpu.SemaphoreType.DMA((9, len(GROUPS))),
            pltpu.SemaphoreType.DMA((9, len(GROUPS))),
            pltpu.SemaphoreType.DMA((ab_rows // LANES,)),
        ],
        name="ladder",
        compiler_params=pltpu.CompilerParams(
            collective_id=0, has_side_effects=True, vmem_limit_bytes=56 << 20
        ),
    )(ab_sizes, cd_sizes, pairs, amplitudes, integrals)


def solution(mesh):
    return jax.shard_map(
        shards,
        mesh=mesh,
        in_specs=(P("ab", "cd"), P("ab", "cd"), P(), P(), P()),
        out_specs=P(None, ("ab", "cd")),
        check_vma=False,
    )
```

time: 275 us -> 108 us (0.39)
  waiting for transfers between devices: 129 us -> 0 us
  Pallas kernels: 0 us -> 103 us
  local copies, waits for them, and re-layouts: 66.6 us -> 3.3 us
  matrix products: 51 us -> 0 us
  between operations: 13.6 us -> 0.02 us
  other arithmetic: 9.8 us -> 0 us
  starting transfers between devices: 4.13 us -> 0 us
    reduce_scatter x1 -> x0, waiting for transfers between devices: 107 us -> none  [sum_over_cd(): return lax.psum_scatter(result, 'cd', scatter_dimension=1, tiled=True)]
    pallas_call x0 -> x1, Pallas kernels: none -> 103 us  [shards(): pl.pallas_call(kernel, out_shape=jax.ShapeDtypeStruct((all_pairs, keeps),...]
    scatter x8 -> x0, local copies, waits for them, and re-layouts: 59.3 us -> none  [shards(): result = result.at[targets].set(block)]
    dot_general x8 -> x0, matrix products: 51 us -> none  [contract(): lax.dot_general(panel, masked, (((1,), (1,)), ((), ())), preferred_elemen...]
    ppermute x7 -> x0, waiting for transfers between devices: 22.2 us -> none  [from_behind(): lax.ppermute(x, axis, [(i, (i + by) % devices) for i in range(devices)])]
    select_n x2 -> x0, other arithmetic: 7.94 us -> none  [the longest x1 7.84 us: shards(): jnp.where(ab_label[:, None] == cd_label[None, :], integrals, jnp.zeros_li...]
    ppermute x7 -> x0, starting transfers between devices: 4.12 us -> none  [from_behind(): lax.ppermute(x, axis, [(i, (i + by) % devices) for i in range(devices)])]
    unnamed x6 -> x1, local copies, waits for them, and re-layouts: 4.66 us -> 1.87 us
  transfers between devices with their start and end apart: 8 -> 0, of which waited for: 7 -> 0; matrix products, arithmetic and copies ran while one was open for 39% -> 0% of each run, Pallas kernels for 0% -> 0%
where the time goes in v1:
time: 108 us; the launch traced here: 107 us
  Pallas kernels  103 us (95%)
  local copies, waits for them, and re-layouts  3.3 us (3%)
    pallas_call x1, Pallas kernels, shards(): pl.pallas_call(kernel, out_shape=jax.ShapeDtypeStruct((all_pairs, keeps),...  103 us

profile of v1, /device:TPU:1, one launch (start us, length us, event | category | flops | bytes accessed | tf_op | source)
XLA Modules:
  0.0 106.7 jit_solution(3518078849272108730)
XLA Ops:
  0.0 0.8 reshape.6
  0.8 0.7 reshape.7.pairs_ref
  1.4 103.4 %ladder.1 = f32[1024,128]{1,0:T(8,128)} custom-call(s32[8]{0:T(128)} %ab_sizes.1, s32[8]{0:T(128)} %cd_sizes.1, s32[8,128]{1,0:T(8,128)} %reshape.7.pairs_ref, bf16[128,3200]{1,0:T(8,128)(2,1)} %amps_ref.1, bf16[2048,3200]{1,0:T(8,128)(2,1)} %ints_ref.1), custom_call_target="tpu_custom_call" | custom-call | tf_op jit(solution)/shard_map/ladder/pallas_call | solution.py:328
  104.8 1.9 %copy.8 = f32[1024,128]{1,0:T(8,128)} copy(f32[1024,128]{1,0:T(8,128)} %ladder.1) | data formatting | bytes 1048576
  (1 shorter events, 0.0 us)

commit v2 on v1

v2 whole, which is shorter than its diff:
```python
import functools

import jax
import jax.numpy as jnp
from jax import lax
from jax.experimental import pallas as pl
from jax.experimental.pallas import tpu as pltpu
from jax.sharding import PartitionSpec as P

MESH = pl.DeviceIdType.MESH
BF16, F32, I32 = jnp.bfloat16, jnp.float32, jnp.int32

PANELS = 8
LANES = 128
CHUNK = 16

CROSS = 8
CUT = 13
CUT_REST = 16

def kernel(
    ab_sizes, cd_sizes, pairs_ref, amps_ref, ints_ref, out_ref,
    amps, ints, prod, from_core, x_one, x_two, from_y, cd_lab,
    g_send, g_recv, r_send, r_recv, local_sem,
):
    panel_rows, depth = amps_ref.shape
    ab_rows = ints_ref.shape[0]
    rounds = panel_rows // CHUNK
    lane_tiles = depth // LANES
    round_rows = PANELS * CHUNK

    ab, cd = lax.axis_index("ab"), lax.axis_index("cd")
    yl, z = ab // 4, lax.rem(ab, 4)
    x, yh, core = cd // 4, lax.rem(cd // 2, 2), lax.rem(cd, 2)
    z_up, z_down, z_far = lax.rem(z + 1, 4), lax.rem(z + 3, 4), lax.rem(z + 2, 4)
    mine, other = yl * 4, (1 - yl) * 4

    to_pair = {"ab": other + z, "cd": cd}
    to_up = {"ab": mine + z_up, "cd": cd}
    to_down = {"ab": mine + z_down, "cd": cd}
    to_core = {"ab": ab, "cd": x * 4 + yh * 2 + (1 - core)}
    to_y = {"ab": ab, "cd": x * 4 + (1 - yh) * 2 + core}
    to_right = {"ab": ab, "cd": lax.rem(x + 1, 4) * 4 + yh * 2 + core}
    to_left = {"ab": ab, "cd": lax.rem(x + 3, 4) * 4 + yh * 2 + core}

    def ints_copy(block):
        k, dc, dy = block // 4, 1 - (block // 2) % 2, block % 2
        dx = 2 + 3 * k - k * (k - 1) // 2
        part = lax.rem(x + dx, 4) * 4 + (yh + dy - 2 * yh * dy) * 2 + (core + dc - 2 * core * dc)
        start = pl.multiple_of(part * LANES, LANES)
        copy = pltpu.make_async_copy(
            ints_ref.at[pl.ds(start, LANES), :],
            ints.at[pl.ds(pl.multiple_of(block * LANES, LANES), LANES), :],
            local_sem.at[block],
        )
        return copy, start

    blocks = ab_rows // LANES

    @pl.loop(0, blocks)
    def _(block):
        ints_copy(block)[0].start()

    barrier = pltpu.get_barrier_semaphore()
    neighbours = (to_pair, to_up, to_down, to_core, to_y, to_right, to_left)
    for neighbour in neighbours:
        pl.semaphore_signal(barrier, inc=1, device_id=neighbour, device_id_type=MESH)
    pl.semaphore_wait(barrier, len(neighbours))

    def slot(q, owner, low, high):
        start = pl.multiple_of(q * round_rows + owner * CHUNK, CHUNK)
        return amps.at[pl.ds(start, CHUNK), pl.ds(low * LANES, (high - low) * LANES)]

    full, cross, rest = (0, lane_tiles), (0, CROSS), (CROSS, lane_tiles)
    low_cut, high_cut = (0, CUT), (CUT, lane_tiles)
    low_rest, high_rest = (CROSS, CUT_REST), (CUT_REST, lane_tiles)
    me, up, down, far = mine + z, mine + z_up, mine + z_down, mine + z_far
    o_me, o_up, o_down, o_far = other + z, other + z_up, other + z_down, other + z_far
    kinds = (
        (me, full, to_pair, o_me),
        (me, full, to_up, down),
        (me, full, to_down, up),
        (o_me, rest, to_up, o_down),
        (o_me, rest, to_down, o_up),
        (down, low_cut, to_up, far),
        (up, high_cut, to_down, far),
        (down, cross, to_pair, o_down),
        (up, cross, to_pair, o_up),
        (o_down, low_rest, to_up, o_far),
        (o_up, high_rest, to_down, o_far),
        (far, cross, to_pair, o_far),
    )

    def g_out(q, kind):
        owner, columns, target, _ = kinds[kind]
        ref = slot(q, owner, *columns)
        own = amps_ref.at[pl.ds(pl.multiple_of(q * CHUNK, CHUNK), CHUNK), :]
        return pltpu.make_async_remote_copy(
            src_ref=own if kind < 3 else ref, dst_ref=ref,
            send_sem=g_send.at[kind, q], recv_sem=g_recv.at[kind, q],
            device_id=target, device_id_type=MESH,
        )

    def g_in(q, kind):
        _, columns, target, owner = kinds[kind]
        ref = slot(q, owner, *columns)
        return pltpu.make_async_remote_copy(
            src_ref=ref, dst_ref=ref, send_sem=g_send.at[kind, q], recv_sem=g_recv.at[kind, q],
            device_id=target, device_id_type=MESH,
        )

    def first(q):
        for kind in (1, 2, 0):
            g_out(q, kind).start()

    def second(q):
        g_in(q, 1).wait_recv()
        g_out(q, 5).start()
        g_out(q, 7).start()
        g_in(q, 2).wait_recv()
        g_out(q, 6).start()
        g_out(q, 8).start()
        g_in(q, 0).wait_recv()
        g_out(q, 3).start()
        g_out(q, 4).start()

    def third(q):
        g_in(q, 5).wait_recv()
        g_out(q, 11).start()
        g_in(q, 3).wait_recv()
        g_out(q, 9).start()
        g_in(q, 4).wait_recv()
        g_out(q, 10).start()

    def arrived(q):
        for kind in (6, 7, 8, 9, 10, 11):
            g_in(q, kind).wait_recv()

    first(0)
    first(1)

    @pl.loop(0, rounds)
    def _(q):
        amps[pl.ds(pl.multiple_of(q * round_rows + me * CHUNK, CHUNK), CHUNK), :] = (
            amps_ref[pl.ds(pl.multiple_of(q * CHUNK, CHUNK), CHUNK), :]
        )

    def ends(sizes):
        out, total = [], jnp.int32(0)
        for k in range(sizes.shape[0]):
            total = total + sizes[k]
            out.append(total)
        return out

    def labels(where_at, limits):
        label = jnp.zeros(where_at.shape, I32)
        for limit in limits:
            label = label + (where_at >= limit).astype(I32)
        return label.astype(F32).astype(BF16)

    ab_ends, cd_ends = ends(ab_sizes), ends(cd_sizes)
    cd_lab[...] = labels(cd * depth + lax.broadcasted_iota(I32, cd_lab.shape, 1), cd_ends)

    def mask(block):
        copy, start = ints_copy(block)
        copy.wait()
        at = lax.broadcasted_iota(I32, (LANES, LANES), 0) + (ab * ab_rows + start)
        ab_lab = labels(at, ab_ends)

        def one(k, carry):
            columns = pl.ds(pl.multiple_of(k * LANES, LANES), LANES)
            rows = pl.ds(pl.multiple_of(block * LANES, LANES), LANES)
            here = jnp.broadcast_to(cd_lab[0:1, columns], (LANES, LANES))
            tile = ints[rows, columns]
            ints[rows, columns] = jnp.where(ab_lab == here, tile, jnp.zeros_like(tile))
            return carry

        lax.fori_loop(0, lane_tiles, one, 0, unroll=5)

    wide = 4 * LANES
    half = 2 * LANES

    def r_copy(g, kind, src, dst, target):
        return pltpu.make_async_remote_copy(
            src_ref=src, dst_ref=dst, send_sem=r_send.at[kind, g], recv_sem=r_recv.at[kind, g],
            device_id=target, device_id_type=MESH,
        )

    def core_copy(g, k):
        src = prod.at[g, pl.ds(pl.multiple_of(k * wide, wide), half), :]
        dst = from_core.at[g, pl.ds(pl.multiple_of(k * half, half), half), :]
        return r_copy(g, k, src, dst, to_core)

    def x_one_copy(g, way):
        src = prod.at[g, pl.ds(half + way * LANES, LANES), :]
        return r_copy(g, 4 + way, src, x_one.at[way, g], (to_right, to_left)[way])

    def x_two_copy(g, way):
        src = prod.at[g, pl.ds((1 + way) * wide + half, half), :]
        return r_copy(g, 6 + way, src, x_two.at[way, g], (to_right, to_left)[way])

    def y_copy(g):
        src = prod.at[g, pl.ds(3 * wide + half + LANES, LANES), :]
        return r_copy(g, 8, src, from_y.at[g], to_y)

    def kept(k):
        return pl.ds(k * wide + half, half)

    def product(g, part):
        columns = pl.ds(pl.multiple_of(part * 2 * wide, 2 * wide), 2 * wide)
        rows = pl.ds(pl.multiple_of(g * round_rows, round_rows), round_rows)
        prod[g, columns, :] = lax.dot_general(
            ints[columns, :], amps[rows, :], (((1,), (1,)), ((), ())), preferred_element_type=F32
        )
        core_copy(g, 2 * part).start()
        core_copy(g, 2 * part + 1).start()

    def x_first(g):
        core_copy(g, 0).wait_recv()
        prod[g, kept(0), :] += from_core[g, pl.ds(0, half), :]
        for way in range(2):
            x_one_copy(g, way).start()

    def x_second(g):
        for way in range(2):
            core_copy(g, 1 + way).wait_recv()
            prod[g, kept(1 + way), :] += from_core[g, pl.ds((1 + way) * half, half), :]
            x_one_copy(g, way).wait_recv()
            prod[g, pl.ds((1 + way) * wide + half + way * LANES, LANES), :] += x_one[way, g]
            x_two_copy(g, way).start()

    def y_step(g):
        core_copy(g, 3).wait_recv()
        total = prod[g, kept(3), :] + from_core[g, pl.ds(3 * half, half), :]
        x_two_copy(g, 0).wait_recv()
        x_two_copy(g, 1).wait_recv()
        prod[g, kept(3), :] = total + x_two[0, g] + x_two[1, g]
        y_copy(g).start()

    def place(g):
        y_copy(g).wait_recv()
        found = prod[g, pl.ds(3 * wide + half, LANES), :] + from_y[g]
        high = found.astype(BF16)
        left = found - high.astype(F32)
        mid = left.astype(BF16)
        low = (left - mid.astype(F32)).astype(BF16)
        target = jnp.broadcast_to(pairs_ref[pl.ds(g, 1), :], out_ref.shape)
        goes = lax.broadcasted_iota(I32, out_ref.shape, 0) == target
        goes = jnp.where(goes, 1.0, 0.0).astype(BF16)
        term = lax.dot_general(
            jnp.concatenate([goes, goes, goes], axis=1), jnp.concatenate([high, mid, low], axis=1),
            (((1,), (1,)), ((), ())), preferred_element_type=F32,
        )
        out_ref[...] += term

    def in_range(step, n):
        pl.when((n >= 0) & (n < rounds))(lambda: step(n))

    out_ref[...] = jnp.zeros_like(out_ref)

    @pl.loop(0, 2 * (rounds + 7))
    def _(h):
        q = h // 2

        @pl.when(h % 2 == 0)
        def _():
            in_range(second, q)
            in_range(first, q + 2)
            in_range(y_step, q - 6)
            in_range(x_first, q - 3)

        @pl.when(h % 2 == 1)
        def _():
            in_range(third, q - 1)
            in_range(arrived, q - 2)
            in_range(x_second, q - 4)
            in_range(place, q - 7)

        @pl.when(h < blocks // 4)
        def _():
            @pl.loop(0, 4)
            def _(block):
                mask(4 * h + block)

        in_range(lambda n: product(n, (h + 1) % 2), (h + 1) // 2 - 3)

    @pl.loop(0, rounds)
    def _(q):
        for kind in range(len(kinds)):
            g_out(q, kind).wait_send()
        for k in range(4):
            core_copy(q, k).wait_send()
        for way in range(2):
            x_one_copy(q, way).wait_send()
            x_two_copy(q, way).wait_send()
        y_copy(q).wait_send()


def shards(amplitudes, integrals, ab_sizes, cd_sizes, pair_index):
    panel_rows, depth = amplitudes.shape
    ab_rows = integrals.shape[0]
    all_pairs = pair_index.shape[0]
    rounds = panel_rows // CHUNK
    keeps = ab_rows // lax.axis_size("cd")
    pairs = pair_index.reshape(PANELS, rounds, CHUNK).transpose(1, 0, 2).reshape(rounds, PANELS * CHUNK)
    vmem, smem = pl.BlockSpec(memory_space=pltpu.VMEM), pl.BlockSpec(memory_space=pltpu.SMEM)
    return pl.pallas_call(
        kernel,
        out_shape=jax.ShapeDtypeStruct((all_pairs, keeps), F32),
        in_specs=[smem, smem, vmem, vmem, pl.BlockSpec(memory_space=pl.ANY)],
        out_specs=vmem,
        scratch_shapes=[
            pltpu.VMEM((all_pairs, depth), BF16),
            pltpu.VMEM((ab_rows, depth), BF16),
            pltpu.VMEM((rounds, ab_rows, PANELS * CHUNK), F32),
            pltpu.VMEM((rounds, ab_rows // 2, PANELS * CHUNK), F32),
            pltpu.VMEM((2, rounds, keeps, PANELS * CHUNK), F32),
            pltpu.VMEM((2, rounds, 2 * keeps, PANELS * CHUNK), F32),
            pltpu.VMEM((rounds, keeps, PANELS * CHUNK), F32),
            pltpu.VMEM((16, depth), BF16),
            pltpu.SemaphoreType.DMA((12, rounds)),
            pltpu.SemaphoreType.DMA((12, rounds)),
            pltpu.SemaphoreType.DMA((9, rounds)),
            pltpu.SemaphoreType.DMA((9, rounds)),
            pltpu.SemaphoreType.DMA((ab_rows // LANES,)),
        ],
        name="ladder",
        compiler_params=pltpu.CompilerParams(
            collective_id=0, has_side_effects=True, vmem_limit_bytes=56 << 20
        ),
    )(ab_sizes, cd_sizes, pairs, amplitudes, integrals)


def solution(mesh):
    return jax.shard_map(
        shards,
        mesh=mesh,
        in_specs=(P("ab", "cd"), P("ab", "cd"), P(), P(), P()),
        out_specs=P(None, ("ab", "cd")),
        check_vma=False,
    )
```

time: 108 us -> 88.9 us (0.82)
  Pallas kernels: 103 us -> 85 us
    pallas_call x1, Pallas kernels: 103 us -> 85 us  [shards(): pl.pallas_call(kernel, out_shape=jax.ShapeDtypeStruct((all_pairs, keeps),...]
where the time goes in v2:
time: 88.9 us; the launch traced here: 88.3 us
  Pallas kernels  85 us (96%)
  local copies, waits for them, and re-layouts  3.3 us (4%)
    pallas_call x1, Pallas kernels, shards(): pl.pallas_call(kernel, out_shape=jax.ShapeDtypeStruct((all_pairs, keeps),...  85 us
    unnamed x1, local copies, waits for them, and re-layouts  1.87 us

profile of v2, /device:TPU:1, one launch (start us, length us, event | category | flops | bytes accessed | tf_op | source)
XLA Modules:
  0.0 88.3 jit_solution(11554885562137903830)
XLA Ops:
  0.0 0.8 reshape.6
  0.8 0.7 reshape.7.pairs_ref
  1.4 85.0 %ladder.1 = f32[1024,128]{1,0:T(8,128)} custom-call(s32[8]{0:T(128)} %ab_sizes.1, s32[8]{0:T(128)} %cd_sizes.1, s32[8,128]{1,0:T(8,128)} %reshape.7.pairs_ref, bf16[128,3200]{1,0:T(8,128)(2,1)} %amps_ref.1, bf16[2048,3200]{1,0:T(8,128)(2,1)} %ints_ref.1), custom_call_target="tpu_custom_call" | custom-call | tf_op jit(solution)/shard_map/ladder/pallas_call | solution.py:307
  86.4 1.9 %copy.8 = f32[1024,128]{1,0:T(8,128)} copy(f32[1024,128]{1,0:T(8,128)} %ladder.1) | data formatting | bytes 1048576
  (1 shorter events, 0.0 us)

commit v3 on v2

--- a/solution.py
+++ b/solution.py
@@ -14,13 +14,35 @@
 LANES = 128
 CHUNK = 16
 
-CROSS = 8
+CROSS = 10
 CUT = 13
-CUT_REST = 16
+CUT_REST = 17
+
+STAGES = (
+    (("third", 1), ("second", 0), ("first", -2), ("y", 5), ("x one", 2)),
+    (("arrived", 1), ("x two", 3), ("place", 6)),
+)
+MULTIPLY = 3
+LATE = 2
+
+def encode(values):
+    largest = jnp.maximum(jnp.max(jnp.abs(values), axis=0, keepdims=True), 1e-30)
+    size = jnp.ceil(jnp.log2(largest) * 16.0) + 1.0
+    codes = jnp.round(values * (jnp.exp2(size * -0.0625) * 32000.0)).astype(I32)
+    sizes = jnp.broadcast_to(size, (CHUNK, values.shape[1])).astype(I32)
+    return jnp.concatenate([codes, sizes], axis=0).astype(jnp.int16)
+
+
+def decode(codes):
+    codes = codes.astype(I32).astype(F32)
+    rows = codes.shape[0] - CHUNK
+    return codes[:rows] * (jnp.exp2(codes[rows : rows + 1] * 0.0625) * (1.0 / 32000.0))
+
 
 def kernel(
     ab_sizes, cd_sizes, pairs_ref, amps_ref, ints_ref, out_ref,
     amps, ints, prod, from_core, x_one, x_two, from_y, cd_lab,
+    x_one_out, x_two_out, y_out,
     g_send, g_recv, r_send, r_recv, local_sem,
 ):
     panel_rows, depth = amps_ref.shape
@@ -192,41 +214,46 @@
         return r_copy(g, k, src, dst, to_core)
 
     def x_one_copy(g, way):
-        src = prod.at[g, pl.ds(half + way * LANES, LANES), :]
-        return r_copy(g, 4 + way, src, x_one.at[way, g], (to_right, to_left)[way])
+        return r_copy(g, 4 + way, x_one_out.at[way, g], x_one.at[way, g], (to_right, to_left)[way])
 
     def x_two_copy(g, way):
-        src = prod.at[g, pl.ds((1 + way) * wide + half, half), :]
-        return r_copy(g, 6 + way, src, x_two.at[way, g], (to_right, to_left)[way])
+        return r_copy(g, 6 + way, x_two_out.at[way, g], x_two.at[way, g], (to_right, to_left)[way])
 
     def y_copy(g):
-        src = prod.at[g, pl.ds(3 * wide + half + LANES, LANES), :]
-        return r_copy(g, 8, src, from_y.at[g], to_y)
+        return r_copy(g, 8, y_out.at[g], from_y.at[g], to_y)
 
     def kept(k):
         return pl.ds(k * wide + half, half)
 
-    def product(g, part):
+    def product(g, part, count):
         columns = pl.ds(pl.multiple_of(part * 2 * wide, 2 * wide), 2 * wide)
-        rows = pl.ds(pl.multiple_of(g * round_rows, round_rows), round_rows)
-        prod[g, columns, :] = lax.dot_general(
+        rows = pl.ds(pl.multiple_of(g * round_rows, round_rows), count * round_rows)
+        found = lax.dot_general(
             ints[columns, :], amps[rows, :], (((1,), (1,)), ((), ())), preferred_element_type=F32
         )
-        core_copy(g, 2 * part).start()
-        core_copy(g, 2 * part + 1).start()
+        for one in range(count):
+            prod[g + one, columns, :] = found[:, one * round_rows : (one + 1) * round_rows]
+        for k in range(2):
+            for one in range(count):
+                core_copy(g + one, 2 * part + k).start()
 
     def x_first(g):
         core_copy(g, 0).wait_recv()
-        prod[g, kept(0), :] += from_core[g, pl.ds(0, half), :]
         for way in range(2):
+            at = half + way * LANES
+            part = prod[g, pl.ds(at, LANES), :] + from_core[g, pl.ds(way * LANES, LANES), :]
+            x_one_out[way, g] = encode(part)
             x_one_copy(g, way).start()
 
     def x_second(g):
         for way in range(2):
             core_copy(g, 1 + way).wait_recv()
-            prod[g, kept(1 + way), :] += from_core[g, pl.ds((1 + way) * half, half), :]
+            part = prod[g, kept(1 + way), :] + from_core[g, pl.ds((1 + way) * half, half), :]
             x_one_copy(g, way).wait_recv()
-            prod[g, pl.ds((1 + way) * wide + half + way * LANES, LANES), :] += x_one[way, g]
+            more = decode(x_one[way, g])
+            low, high = part[:LANES], part[LANES:]
+            low, high = (low, high + more) if way else (low + more, high)
+            x_two_out[way, g] = encode(jnp.concatenate([low, high], axis=0))
             x_two_copy(g, way).start()
 
     def y_step(g):
@@ -234,18 +261,21 @@
         total = prod[g, kept(3), :] + from_core[g, pl.ds(3 * half, half), :]
         x_two_copy(g, 0).wait_recv()
         x_two_copy(g, 1).wait_recv()
-        prod[g, kept(3), :] = total + x_two[0, g] + x_two[1, g]
+        total = total + decode(x_two[0, g]) + decode(x_two[1, g])
+        y_out[g] = encode(total[LANES:])
         y_copy(g).start()
+        prod[g, pl.ds(3 * wide + half, LANES), :] = total[:LANES]
 
     def place(g):
         y_copy(g).wait_recv()
-        found = prod[g, pl.ds(3 * wide + half, LANES), :] + from_y[g]
+        found = prod[g, pl.ds(3 * wide + half, LANES), :] + decode(from_y[g])
         high = found.astype(BF16)
         left = found - high.astype(F32)
         mid = left.astype(BF16)
         low = (left - mid.astype(F32)).astype(BF16)
-        target = jnp.broadcast_to(pairs_ref[pl.ds(g, 1), :], out_ref.shape)
-        goes = lax.broadcasted_iota(I32, out_ref.shape, 0) == target
+        shape = (out_ref.shape[0], round_rows)
+        target = jnp.broadcast_to(pairs_ref[pl.ds(g, 1), :], shape)
+        goes = lax.broadcasted_iota(I32, shape, 0) == target
         goes = jnp.where(goes, 1.0, 0.0).astype(BF16)
         term = lax.dot_general(
             jnp.concatenate([goes, goes, goes], axis=1), jnp.concatenate([high, mid, low], axis=1),
@@ -256,25 +286,35 @@
     def in_range(step, n):
         pl.when((n >= 0) & (n < rounds))(lambda: step(n))
 
+    late = rounds - LATE
+
+    def together(step, n):
+        @pl.when((n >= 0) & (n < rounds) & ((n >= late) | (n % 2 == 1)))
+        def _():
+            pl.loop(n - (n < late).astype(I32), n + 1)(step)
+
+    does = {
+        "first": functools.partial(in_range, first),
+        "second": functools.partial(in_range, second),
+        "third": functools.partial(in_range, third),
+        "arrived": functools.partial(in_range, arrived),
+        "x one": functools.partial(together, x_first),
+        "x two": functools.partial(together, x_second),
+        "y": functools.partial(together, y_step),
+        "place": functools.partial(together, place),
+    }
     out_ref[...] = jnp.zeros_like(out_ref)
 
     @pl.loop(0, 2 * (rounds + 7))
     def _(h):
         q = h // 2
 
-        @pl.when(h % 2 == 0)
-        def _():
-            in_range(second, q)
-            in_range(first, q + 2)
-            in_range(y_step, q - 6)
-            in_range(x_first, q - 3)
-
-        @pl.when(h % 2 == 1)
-        def _():
-            in_range(third, q - 1)
-            in_range(arrived, q - 2)
-            in_range(x_second, q - 4)
-            in_range(place, q - 7)
+        for parity in range(2):
+
+            @pl.when(h % 2 == parity)
+            def _():
+                for name, lag in STAGES[parity]:
+                    does[name](q - lag)
 
         @pl.when(h < blocks // 4)
         def _():
@@ -282,7 +322,15 @@
             def _(block):
                 mask(4 * h + block)
 
-        in_range(lambda n: product(n, (h + 1) % 2), (h + 1) // 2 - 3)
+        ready, part = (h + 8 - MULTIPLY) // 2 - 4, (h + 8 - MULTIPLY) % 2
+
+        @pl.when((ready >= late) & (ready < rounds))
+        def _():
+            product(ready, part, 1)
+
+        @pl.when((ready >= 0) & (ready < late) & (ready % 2 == 1))
+        def _():
+            product(ready - 1, part, 2)
 
     @pl.loop(0, rounds)
     def _(q):
@@ -303,6 +351,11 @@
     rounds = panel_rows // CHUNK
     keeps = ab_rows // lax.axis_size("cd")
     pairs = pair_index.reshape(PANELS, rounds, CHUNK).transpose(1, 0, 2).reshape(rounds, PANELS * CHUNK)
+    sums = (
+        pltpu.VMEM((2, rounds, keeps + CHUNK, PANELS * CHUNK), jnp.int16),
+        pltpu.VMEM((2, rounds, 2 * keeps + CHUNK, PANELS * CHUNK), jnp.int16),
+        pltpu.VMEM((rounds, keeps + CHUNK, PANELS * CHUNK), jnp.int16),
+    )
     vmem, smem = pl.BlockSpec(memory_space=pltpu.VMEM), pl.BlockSpec(memory_space=pltpu.SMEM)
     return pl.pallas_call(
         kernel,
@@ -314,10 +367,9 @@
             pltpu.VMEM((ab_rows, depth), BF16),
             pltpu.VMEM((rounds, ab_rows, PANELS * CHUNK), F32),
             pltpu.VMEM((rounds, ab_rows // 2, PANELS * CHUNK), F32),
-            pltpu.VMEM((2, rounds, keeps, PANELS * CHUNK), F32),
-            pltpu.VMEM((2, rounds, 2 * keeps, PANELS * CHUNK), F32),
-            pltpu.VMEM((rounds, keeps, PANELS * CHUNK), F32),
+            *sums,
             pltpu.VMEM((16, depth), BF16),
+            *sums,
             pltpu.SemaphoreType.DMA((12, rounds)),
             pltpu.SemaphoreType.DMA((12, rounds)),
             pltpu.SemaphoreType.DMA((9, rounds)),

time: 88.9 us -> 83.9 us (0.944)
  Pallas kernels: 85 us -> 80.4 us
    pallas_call x1, Pallas kernels: 85 us -> 80.4 us  [shards(): pl.pallas_call(kernel, out_shape=jax.ShapeDtypeStruct((all_pairs, keeps),...]
where the time goes in v3:
time: 83.9 us; the launch traced here: 83.7 us
  Pallas kernels  80.4 us (96%)
  local copies, waits for them, and re-layouts  3.3 us (4%)
    pallas_call x1, Pallas kernels, shards(): pl.pallas_call(kernel, out_shape=jax.ShapeDtypeStruct((all_pairs, keeps),...  80.4 us
    unnamed x1, local copies, waits for them, and re-layouts  1.87 us

profile of v3, /device:TPU:1, one launch (start us, length us, event | category | flops | bytes accessed | tf_op | source)
XLA Modules:
  0.0 83.7 jit_solution(6860894056408309238)
XLA Ops:
  0.0 0.8 reshape.6
  0.8 0.7 reshape.7.pairs_ref
  1.4 80.4 %ladder.1 = f32[1024,128]{1,0:T(8,128)} custom-call(s32[8]{0:T(128)} %ab_sizes.1, s32[8]{0:T(128)} %cd_sizes.1, s32[8,128]{1,0:T(8,128)} %reshape.7.pairs_ref, bf16[128,3200]{1,0:T(8,128)(2,1)} %amps_ref.1, bf16[2048,3200]{1,0:T(8,128)(2,1)} %ints_ref.1), custom_call_target="tpu_custom_call" | custom-call | tf_op jit(solution)/shard_map/ladder/pallas_call | solution.py:360
  81.8 1.9 %copy.8 = f32[1024,128]{1,0:T(8,128)} copy(f32[1024,128]{1,0:T(8,128)} %ladder.1) | data formatting | bytes 1048576
  (1 shorter events, 0.0 us)

commit v4 on v3

--- a/solution.py
+++ b/solution.py
@@ -42,7 +42,7 @@
 def kernel(
     ab_sizes, cd_sizes, pairs_ref, amps_ref, ints_ref, out_ref,
     amps, ints, prod, from_core, x_one, x_two, from_y, cd_lab,
-    x_one_out, x_two_out, y_out,
+    x_one_out, x_two_out, y_out, targets,
     g_send, g_recv, r_send, r_recv, local_sem,
 ):
     panel_rows, depth = amps_ref.shape
@@ -155,17 +155,23 @@
         g_out(q, 10).start()
 
     def arrived(q):
+        own_copy(q).wait()
         for kind in (6, 7, 8, 9, 10, 11):
             g_in(q, kind).wait_recv()
 
+    def own_copy(q):
+        return pltpu.make_async_copy(
+            amps_ref.at[pl.ds(pl.multiple_of(q * CHUNK, CHUNK), CHUNK), :],
+            slot(q, me, *full),
+            local_sem.at[blocks + q],
+        )
+
     first(0)
     first(1)
 
     @pl.loop(0, rounds)
     def _(q):
-        amps[pl.ds(pl.multiple_of(q * round_rows + me * CHUNK, CHUNK), CHUNK), :] = (
-            amps_ref[pl.ds(pl.multiple_of(q * CHUNK, CHUNK), CHUNK), :]
-        )
+        own_copy(q).start()
 
     def ends(sizes):
         out, total = [], jnp.int32(0)
@@ -274,7 +280,7 @@
         mid = left.astype(BF16)
         low = (left - mid.astype(F32)).astype(BF16)
         shape = (out_ref.shape[0], round_rows)
-        target = jnp.broadcast_to(pairs_ref[pl.ds(g, 1), :], shape)
+        target = jnp.broadcast_to(targets[pl.ds(g, 1), :], shape)
         goes = lax.broadcasted_iota(I32, shape, 0) == target
         goes = jnp.where(goes, 1.0, 0.0).astype(BF16)
         term = lax.dot_general(
@@ -282,6 +288,24 @@
             (((1,), (1,)), ((), ())), preferred_element_type=F32,
         )
         out_ref[...] += term
+        for kind in range(len(kinds)):
+            g_out(g, kind).wait_send()
+        for k in range(4):
+            core_copy(g, k).wait_send()
+        for way in range(2):
+            x_one_copy(g, way).wait_send()
+            x_two_copy(g, way).wait_send()
+        y_copy(g).wait_send()
+
+    pairs = pairs_ref[...]
+    chunk = lax.broadcasted_iota(I32, pairs.shape, 1) // CHUNK
+    panel = lax.broadcasted_iota(I32, pairs.shape, 0)
+    turned = [pairs if m == 0 else pltpu.roll(pairs, m * CHUNK, 1) for m in range(rounds)]
+    for g in range(rounds):
+        chosen = jnp.zeros_like(pairs)
+        for p in range(PANELS):
+            chosen = jnp.where((panel == p) & (chunk == p), turned[(p - g) % rounds], chosen)
+        targets[g : g + 1, :] = jnp.sum(chosen, axis=0, keepdims=True)
 
     def in_range(step, n):
         pl.when((n >= 0) & (n < rounds))(lambda: step(n))
@@ -332,17 +356,6 @@
         def _():
             product(ready - 1, part, 2)
 
-    @pl.loop(0, rounds)
-    def _(q):
-        for kind in range(len(kinds)):
-            g_out(q, kind).wait_send()
-        for k in range(4):
-            core_copy(q, k).wait_send()
-        for way in range(2):
-            x_one_copy(q, way).wait_send()
-            x_two_copy(q, way).wait_send()
-        y_copy(q).wait_send()
-
 
 def shards(amplitudes, integrals, ab_sizes, cd_sizes, pair_index):
     panel_rows, depth = amplitudes.shape
@@ -350,17 +363,18 @@
     all_pairs = pair_index.shape[0]
     rounds = panel_rows // CHUNK
     keeps = ab_rows // lax.axis_size("cd")
-    pairs = pair_index.reshape(PANELS, rounds, CHUNK).transpose(1, 0, 2).reshape(rounds, PANELS * CHUNK)
+    pairs = pair_index.reshape(PANELS, panel_rows)
     sums = (
         pltpu.VMEM((2, rounds, keeps + CHUNK, PANELS * CHUNK), jnp.int16),
         pltpu.VMEM((2, rounds, 2 * keeps + CHUNK, PANELS * CHUNK), jnp.int16),
         pltpu.VMEM((rounds, keeps + CHUNK, PANELS * CHUNK), jnp.int16),
     )
     vmem, smem = pl.BlockSpec(memory_space=pltpu.VMEM), pl.BlockSpec(memory_space=pltpu.SMEM)
+    hbm = pl.BlockSpec(memory_space=pl.ANY)
     return pl.pallas_call(
         kernel,
         out_shape=jax.ShapeDtypeStruct((all_pairs, keeps), F32),
-        in_specs=[smem, smem, vmem, vmem, pl.BlockSpec(memory_space=pl.ANY)],
+        in_specs=[smem, smem, vmem, hbm, hbm],
         out_specs=vmem,
         scratch_shapes=[
             pltpu.VMEM((all_pairs, depth), BF16),
@@ -370,11 +384,12 @@
             *sums,
             pltpu.VMEM((16, depth), BF16),
             *sums,
+            pltpu.VMEM((rounds, PANELS * CHUNK), I32),
             pltpu.SemaphoreType.DMA((12, rounds)),
             pltpu.SemaphoreType.DMA((12, rounds)),
             pltpu.SemaphoreType.DMA((9, rounds)),
             pltpu.SemaphoreType.DMA((9, rounds)),
-            pltpu.SemaphoreType.DMA((ab_rows // LANES,)),
+            pltpu.SemaphoreType.DMA((ab_rows // LANES + rounds,)),
         ],
         name="ladder",
         compiler_params=pltpu.CompilerParams(

time: 83.9 us -> 82.1 us (0.979)
  local copies, waits for them, and re-layouts: 3.3 us -> 1.87 us
    reshape x2 -> x0, local copies, waits for them, and re-layouts: 1.43 us -> none  [shards(): pair_index.reshape(PANELS, rounds, CHUNK).transpose(1, 0, 2)]
where the time goes in v4:
time: 82.1 us; the launch traced here: 81.9 us
  Pallas kernels  80 us (97%)
  local copies, waits for them, and re-layouts  1.87 us (2%)
    pallas_call x1, Pallas kernels, shards(): pl.pallas_call(kernel, out_shape=jax.ShapeDtypeStruct((all_pairs, keeps),...  80 us
    unnamed x1, local copies, waits for them, and re-layouts  1.87 us

profile of v4, /device:TPU:1, one launch (start us, length us, event | category | flops | bytes accessed | tf_op | source)
XLA Modules:
  0.0 81.9 jit_solution(11516417479819262287)
XLA Ops:
  0.0 80.0 %ladder.1 = f32[1024,128]{1,0:T(8,128)} custom-call(s32[8]{0:T(128)} %ab_sizes.1, s32[8]{0:T(128)} %cd_sizes.1, s32[8,128]{1,0:T(8,128)} %bitcast.1, bf16[128,3200]{1,0:T(8,128)(2,1)} %amps_ref.1, bf16[2048,3200]{1,0:T(8,128)(2,1)} %ints_ref.1), custom_call_target="tpu_custom_call" | custom-call | tf_op jit(solution)/shard_map/ladder/pallas_call | solution.py:374
  80.1 1.9 %copy.7 = f32[1024,128]{1,0:T(8,128)} copy(f32[1024,128]{1,0:T(8,128)} %ladder.1) | data formatting | bytes 1048576

commit v5 on v4

--- a/solution.py
+++ b/solution.py
@@ -19,10 +19,11 @@
 CUT_REST = 17
 
 STAGES = (
-    (("third", 1), ("second", 0), ("first", -2), ("y", 5), ("x one", 2)),
-    (("arrived", 1), ("x two", 3), ("place", 6)),
+    (("third", 1), ("second", 0), ("first", -2), ("y", 6), ("x one", 2)),
+    (("arrived", 1), ("x two", 3), ("place", 8)),
 )
 MULTIPLY = 3
+DRAIN = 8
 LATE = 2
 
 def encode(values):
@@ -273,16 +274,16 @@
         prod[g, pl.ds(3 * wide + half, LANES), :] = total[:LANES]
 
     def place(g):
+        shape = (out_ref.shape[0], round_rows)
+        target = jnp.broadcast_to(targets[pl.ds(g, 1), :], shape)
+        goes = lax.broadcasted_iota(I32, shape, 0) == target
+        goes = jnp.where(goes, 1.0, 0.0).astype(BF16)
         y_copy(g).wait_recv()
         found = prod[g, pl.ds(3 * wide + half, LANES), :] + decode(from_y[g])
         high = found.astype(BF16)
         left = found - high.astype(F32)
         mid = left.astype(BF16)
         low = (left - mid.astype(F32)).astype(BF16)
-        shape = (out_ref.shape[0], round_rows)
-        target = jnp.broadcast_to(targets[pl.ds(g, 1), :], shape)
-        goes = lax.broadcasted_iota(I32, shape, 0) == target
-        goes = jnp.where(goes, 1.0, 0.0).astype(BF16)
         term = lax.dot_general(
             jnp.concatenate([goes, goes, goes], axis=1), jnp.concatenate([high, mid, low], axis=1),
             (((1,), (1,)), ((), ())), preferred_element_type=F32,
@@ -329,7 +330,7 @@
     }
     out_ref[...] = jnp.zeros_like(out_ref)
 
-    @pl.loop(0, 2 * (rounds + 7))
+    @pl.loop(0, 2 * (rounds + DRAIN))
     def _(h):
         q = h // 2
 
@@ -373,7 +374,7 @@
     hbm = pl.BlockSpec(memory_space=pl.ANY)
     return pl.pallas_call(
         kernel,
-        out_shape=jax.ShapeDtypeStruct((all_pairs, keeps), F32),
+        out_shape=pltpu.VMEM((all_pairs, keeps), F32),
         in_specs=[smem, smem, vmem, hbm, hbm],
         out_specs=vmem,
         scratch_shapes=[

time: 82.1 us -> 79.1 us (0.963)
  Pallas kernels: 80 us -> 78.2 us
  local copies, waits for them, and re-layouts: 1.87 us -> 0.8 us
    pallas_call x1, Pallas kernels: 80 us -> 78.2 us  [shards(): pl.pallas_call(kernel, out_shape=pltpu.VMEM((all_pairs, keeps), F32), in_...]
    unnamed x1, local copies, waits for them, and re-layouts: 1.87 us -> 0.8 us
where the time goes in v5:
time: 79.1 us; the launch traced here: 79 us
  Pallas kernels  78.2 us (99%)
  local copies, waits for them, and re-layouts  0.8 us (1%)
    pallas_call x1, Pallas kernels, shards(): pl.pallas_call(kernel, out_shape=pltpu.VMEM((all_pairs, keeps), F32), in_...  78.2 us

profile of v5, /device:TPU:1, one launch (start us, length us, event | category | flops | bytes accessed | tf_op | source)
XLA Modules:
  0.0 79.0 jit_solution(4580599926564782777)
XLA Ops:
  0.0 78.2 %ladder.1 = f32[1024,128]{1,0:T(8,128)S(1)} custom-call(s32[8]{0:T(128)} %ab_sizes.1, s32[8]{0:T(128)} %cd_sizes.1, s32[8,128]{1,0:T(8,128)} %bitcast.1, bf16[128,3200]{1,0:T(8,128)(2,1)} %amps_ref.1, bf16[2048,3200]{1,0:T(8,128)(2,1)} %ints_ref.1), custom_call_target="tpu_custom_call" | custom-call | tf_op jit(solution)/shard_map/ladder/pallas_call | solution.py:375
  78.2 0.8 %copy.7 = f32[1024,128]{1,0:T(8,128)} copy(f32[1024,128]{1,0:T(8,128)S(1)} %ladder.1) | data formatting | bytes 1048576

commit v6 on v5

--- a/solution.py
+++ b/solution.py
@@ -66,6 +66,11 @@
     to_right = {"ab": ab, "cd": lax.rem(x + 1, 4) * 4 + yh * 2 + core}
     to_left = {"ab": ab, "cd": lax.rem(x + 3, 4) * 4 + yh * 2 + core}
 
+    barrier = pltpu.get_barrier_semaphore()
+    neighbours = (to_pair, to_up, to_down, to_core, to_y, to_right, to_left)
+    for neighbour in neighbours:
+        pl.semaphore_signal(barrier, inc=1, device_id=neighbour, device_id_type=MESH)
+
     def ints_copy(block):
         k, dc, dy = block // 4, 1 - (block // 2) % 2, block % 2
         dx = 2 + 3 * k - k * (k - 1) // 2
@@ -84,10 +89,6 @@
     def _(block):
         ints_copy(block)[0].start()
 
-    barrier = pltpu.get_barrier_semaphore()
-    neighbours = (to_pair, to_up, to_down, to_core, to_y, to_right, to_left)
-    for neighbour in neighbours:
-        pl.semaphore_signal(barrier, inc=1, device_id=neighbour, device_id_type=MESH)
     pl.semaphore_wait(barrier, len(neighbours))
 
     def slot(q, owner, low, high):

time: 79.1 us -> 78.6 us (level)
  no operation moved by 1% of the time
where the time goes in v6:
time: 78.6 us; the launch traced here: 78.5 us
  Pallas kernels  77.7 us (99%)
  local copies, waits for them, and re-layouts  0.8 us (1%)
    pallas_call x1, Pallas kernels, shards(): pl.pallas_call(kernel, out_shape=pltpu.VMEM((all_pairs, keeps), F32), in_...  77.7 us

profile of v6, /device:TPU:1, one launch (start us, length us, event | category | flops | bytes accessed | tf_op | source)
XLA Modules:
  0.0 78.5 jit_solution(9629845552756106373)
XLA Ops:
  0.0 77.7 %ladder.1 = f32[1024,128]{1,0:T(8,128)S(1)} custom-call(s32[8]{0:T(128)} %ab_sizes.1, s32[8]{0:T(128)} %cd_sizes.1, s32[8,128]{1,0:T(8,128)} %bitcast.1, bf16[128,3200]{1,0:T(8,128)(2,1)} %amps_ref.1, bf16[2048,3200]{1,0:T(8,128)(2,1)} %ints_ref.1), custom_call_target="tpu_custom_call" | custom-call | tf_op jit(solution)/shard_map/ladder/pallas_call | solution.py:376
  77.7 0.8 %copy.7 = f32[1024,128]{1,0:T(8,128)} copy(f32[1024,128]{1,0:T(8,128)S(1)} %ladder.1) | data formatting | bytes 1048576
